TPU v7x, 128 devices: a whole 4x4x4 slice. The times are simulated.
128 devices in a mesh: leaf: 64 (over z, y, x), rep: 2 (over core).
Axes of the slice: x: 4, y: 4, z: 4, core: 2. Of those that a mesh axis runs over, the one named last changes fastest.
Arguments:
- queries: bfloat16 [16384, 3584], P(('rep', 'leaf')), parts along dimension 0, may hold values from -64 to 64
- branch_key_value: bfloat16 [2, 16384, 512], P(None, ('rep', 'leaf')), parts along dimension 1, may hold values from -5 to 5
- prompt_key_value: bfloat16 [2, 16384, 512], P(None, ('rep', 'leaf')), parts along dimension 1, may hold values from -5 to 5
- parents: int32 [128], P('rep'), parts along dimension 0, may hold values from -1 to 62, as said below
- counts: int32 [128], P('rep'), parts along dimension 0, may hold values from 1 to 128, as said below
Outputs:
- attended: bfloat16 [16384, 3584], P(('rep', 'leaf')), parts along dimension 0
There are 2 independent parts, one for each index of `rep`. A program takes and returns all parts, laid end to end along the dimension named above; each array names one. Nothing has to cross between parts.
Inputs may be any that keep to these rules, and one draw needn't show every extreme that they name: parents[b] is below b; parents[b] is -1 or at least 4 * (b // 4), so every tree lies within one aligned run of 4 blocks; the last block of every such run has the run's first block as parent; parents[0] is -1. counts[0] is 128.
All inputs are finite; a program needn't handle non-finite values.
Results may differ from a plain program's by a relative error of at most 0.0095.
Values may be sent and summed in bfloat16 or wider, within the bound.
A program may use at most 320 MiB of HBM per device.

v0:
```python
import jax
import jax.numpy as jnp
from jax import lax
from jax.sharding import PartitionSpec as P

QUERY_HEADS = 28
KEY_VALUE_HEADS = 4
HEAD_SIZE = 128
BLOCK_TOKENS = 128
REACH = 4


def attend_piece(state, block_portion, seen, query_head_rows):
    running, total, summed = state
    token_length = block_portion.shape[1]
    current_keys = block_portion[0].reshape(token_length, KEY_VALUE_HEADS, HEAD_SIZE)
    current_values = block_portion[1].reshape(token_length, KEY_VALUE_HEADS, HEAD_SIZE)
    scores = jnp.einsum(
        "rkgd,nkd->rkgn", query_head_rows, current_keys, preferred_element_type=jnp.float32
    ) * HEAD_SIZE ** (-0.5)
    scores = jnp.where(seen[:, None, None, :], scores, -1e30)
    newest = jnp.maximum(running, jnp.max(scores, axis=-1))
    factor = jnp.exp(running - newest)
    expo = jnp.where(seen[:, None, None, :], jnp.exp(scores - newest[..., None]), 0.0)
    total = total * factor + jnp.sum(expo, axis=-1)
    product = jnp.einsum(
        "rkgn,nkd->rkgd",
        expo.astype(jnp.bfloat16),
        current_values,
        preferred_element_type=jnp.float32,
    )
    summed = summed * factor[..., None] + product
    return (newest, total, summed)


def shards(queries, branch_key_value, prompt_key_value, parents, counts):
    total_blocks = parents.shape[0]
    nearby_rows = queries.shape[0]
    group_index = QUERY_HEADS // KEY_VALUE_HEADS
    block_index = jnp.arange(total_blocks, dtype=jnp.int32)
    query_head_rows = queries.reshape(nearby_rows, KEY_VALUE_HEADS, group_index, HEAD_SIZE)
    device = lax.axis_index("leaf")
    query_slot = device * nearby_rows + jnp.arange(nearby_rows, dtype=jnp.int32)
    query_block = query_slot // BLOCK_TOKENS
    query_pos = query_slot % BLOCK_TOKENS
    chain_steps = REACH * (nearby_rows // BLOCK_TOKENS + 0) + REACH

    def climb(step, state):
        marked, current = state
        marked = marked | (current[:, None] == block_index[None, :])
        current = jnp.where(current >= 0, parents[jnp.maximum(current, 0)], -1)
        return (marked, current)

    start_marks = jnp.zeros((nearby_rows, total_blocks), dtype=bool)
    query_table, unused_current = lax.fori_loop(
        0, chain_steps, climb, (start_marks, parents[query_block])
    )

    def tree_seen(start, token_length):
        key_slot = start + jnp.arange(token_length, dtype=jnp.int32)
        key_block = key_slot // BLOCK_TOKENS
        key_pos = key_slot % BLOCK_TOKENS
        key_count = counts[key_block]
        linked = jnp.take(query_table, key_block, axis=1)
        linked = linked & (key_pos < key_count)[None, :]
        own = (query_block[:, None] == key_block[None, :]) & (
            key_pos[None, :] <= query_pos[:, None]
        )
        return linked | own

    def root_step(state, block_portion, start):
        seen = jnp.ones((nearby_rows, block_portion.shape[1]), dtype=bool)
        return attend_piece(state, block_portion, seen, query_head_rows)

    def tree_step(state, block_portion, start):
        return attend_piece(
            state, block_portion, tree_seen(start, block_portion.shape[1]), query_head_rows
        )

    initial = (
        jnp.full((nearby_rows, KEY_VALUE_HEADS, group_index), -1e30, jnp.float32),
        jnp.zeros((nearby_rows, KEY_VALUE_HEADS, group_index), jnp.float32),
        jnp.zeros((nearby_rows, KEY_VALUE_HEADS, group_index, HEAD_SIZE), jnp.float32),
    )
    root_whole, tree_whole = (
        lax.all_gather(prompt_key_value, "leaf", axis=1, tiled=True),
        lax.all_gather(branch_key_value, "leaf", axis=1, tiled=True),
    )

    def sweep(state, whole, step_fn):
        token_length = whole.shape[1]
        width = min(512, token_length)
        pieces = token_length // width
        stacked = whole.reshape(2, pieces, width, whole.shape[2]).transpose(1, 0, 2, 3)
        starts = jnp.arange(pieces, dtype=jnp.int32) * width

        def inner(carry, item):
            block_portion, start = item
            return (step_fn(carry, block_portion, start), None)

        state, unused = lax.scan(inner, state, (stacked, starts))
        return state

    state = sweep(initial, root_whole, root_step)
    state = sweep(state, tree_whole, tree_step)
    running, total, summed = state
    result = summed / total[..., None]
    live = query_pos < counts[query_block]
    result = jnp.where(live[:, None, None, None], result, 0.0)
    return result.reshape(nearby_rows, QUERY_HEADS * HEAD_SIZE).astype(jnp.bfloat16)


def solution(mesh):
    placed = (
        P(("rep", "leaf"), None),
        P(None, ("rep", "leaf"), None),
        P(None, ("rep", "leaf"), None),
        P("rep"),
        P("rep"),
    )
    return jax.shard_map(
        shards, mesh=mesh, in_specs=placed, out_specs=P(("rep", "leaf"), None), check_vma=False
    )
```

profile of v0, /device:TPU:0, one launch (start us, length us, event | category | flops | bytes accessed | tf_op | source)
XLA Modules:
  0.0 1446.0 jit_solution(7694382927498422993)
XLA Ops:
  13.5 13.9 while.47
  28.8 88.4 %all-gather.3.cloned.1.call-done = bf16[2,8192,512]{2,1,0:T(8,128)(2,1)} async-done(((bf16[2,128,512]{2,1,0:T(8,128)(2,1)}), bf16[2,8192,512]{2,1,0:T(8,128)(2,1)}) %all-gather.3.cloned.1.call-update) | async-done | bytes 16777232 | tf_op jit(solution)/shard_map/all_gather | solution.py:86
  117.1 295.9 %while.46 = (s32[]{:T(128)}, f32[128,4,7]{0,2,1:T(8,128)S(1)}, f32[128,4,7]{0,2,1:T(8,128)S(1)}, f32[128,4,7,128]{0,3,2,1:T(8,128)S(1)}, bf16[16,2,512,512]{3,2,...) while((s32[]{:T(128)}, f32[128,4,7]{0,2,1:T(8,128)S(1)}, ...), condition=%wide.region_3.4_spmd.clone, body=%wide.region_0.3_spmd.clone.sunk | while | flops 955598336 | bytes 32079996 | solution.py:101
  130.4 5.2 bitcast_add_fusion.4
  148.9 5.4 bitcast_add_fusion.4
  167.8 5.1 bitcast_add_fusion.4
  186.4 5.5 bitcast_add_fusion.4
  205.3 5.4 bitcast_add_fusion.4
  224.0 5.1 bitcast_add_fusion.4
  242.4 5.1 bitcast_add_fusion.4
  260.8 5.1 bitcast_add_fusion.4
  334.3 5.1 bitcast_add_fusion.4
  352.7 5.1 bitcast_add_fusion.4
  371.1 5.1 bitcast_add_fusion.4
  389.5 5.1 bitcast_add_fusion.4
  413.0 1024.6 %while.48 = (s32[]{:T(128)}, f32[128,4,7]{0,2,1:T(8,128)S(1)}, f32[128,4,7]{0,2,1:T(8,128)S(1)}, f32[128,4,7,128]{0,3,2,1:T(8,128)S(1)}, s32[16]{0:T(128)S(1)}, ...) while((s32[]{:T(128)}, f32[128,4,7]{0,2,1:T(8,128)S(1)}, ...), condition=%wide.region_9.10_spmd.clone.clone, body=%wide.region_6.9_spmd.clone.clone.sunk | while | flops 964803072 | bytes 64021480 | solution.py:101
  417.4 40.6 %select_compare_fusion.2 = pred[512]{0:T(512)(128)(4,1)S(1)} fusion(s32[512]{0:T(512)S(1)} %bitcast.311, s32[]{:T(128)} %bitcast.237, s32[]{:T(128)} %bitcast.238, s32[]{:T(128)} %bitcast.239, s32[]{:T(128)} %bitcast.240, s32[]{:T(128)} %bitcast.241, s32[]{:T(128)} %bitcast.242, s32[]{:T(128)} %bitcast.243, s32[]{:T(128)} %bitcast.244, s32[]{:T(128)} %bitcast.245, ...), kind=kLoop, calls=%fused_computation.52.clone.1 | loop fusion | flops 71168 | bytes 2820 | tf_op jit(solution)/shard_map/while/body/eval_jaxpr/lt | solution.py:65
  471.5 5.7 bitcast_add_fusion.5
  481.4 40.6 %select_compare_fusion.2 = pred[512]{0:T(512)(128)(4,1)S(1)} fusion(s32[512]{0:T(512)S(1)} %bitcast.311, s32[]{:T(128)} %bitcast.237, s32[]{:T(128)} %bitcast.238, s32[]{:T(128)} %bitcast.239, s32[]{:T(128)} %bitcast.240, s32[]{:T(128)} %bitcast.241, s32[]{:T(128)} %bitcast.242, s32[]{:T(128)} %bitcast.243, s32[]{:T(128)} %bitcast.244, s32[]{:T(128)} %bitcast.245, ...), kind=kLoop, calls=%fused_computation.52.clone.1 | loop fusion | flops 71168 | bytes 2820 | tf_op jit(solution)/shard_map/while/body/eval_jaxpr/lt | solution.py:65
  535.6 5.7 bitcast_add_fusion.5
  545.4 40.6 %select_compare_fusion.2 = pred[512]{0:T(512)(128)(4,1)S(1)} fusion(s32[512]{0:T(512)S(1)} %bitcast.311, s32[]{:T(128)} %bitcast.237, s32[]{:T(128)} %bitcast.238, s32[]{:T(128)} %bitcast.239, s32[]{:T(128)} %bitcast.240, s32[]{:T(128)} %bitcast.241, s32[]{:T(128)} %bitcast.242, s32[]{:T(128)} %bitcast.243, s32[]{:T(128)} %bitcast.244, s32[]{:T(128)} %bitcast.245, ...), kind=kLoop, calls=%fused_computation.52.clone.1 | loop fusion | flops 71168 | bytes 2820 | tf_op jit(solution)/shard_map/while/body/eval_jaxpr/lt | solution.py:65
  599.6 5.7 bitcast_add_fusion.5
  609.4 40.6 %select_compare_fusion.2 = pred[512]{0:T(512)(128)(4,1)S(1)} fusion(s32[512]{0:T(512)S(1)} %bitcast.311, s32[]{:T(128)} %bitcast.237, s32[]{:T(128)} %bitcast.238, s32[]{:T(128)} %bitcast.239, s32[]{:T(128)} %bitcast.240, s32[]{:T(128)} %bitcast.241, s32[]{:T(128)} %bitcast.242, s32[]{:T(128)} %bitcast.243, s32[]{:T(128)} %bitcast.244, s32[]{:T(128)} %bitcast.245, ...), kind=kLoop, calls=%fused_computation.52.clone.1 | loop fusion | flops 71168 | bytes 2820 | tf_op jit(solution)/shard_map/while/body/eval_jaxpr/lt | solution.py:65
  663.6 5.7 bitcast_add_fusion.5
  673.5 40.6 %select_compare_fusion.2 = pred[512]{0:T(512)(128)(4,1)S(1)} fusion(s32[512]{0:T(512)S(1)} %bitcast.311, s32[]{:T(128)} %bitcast.237, s32[]{:T(128)} %bitcast.238, s32[]{:T(128)} %bitcast.239, s32[]{:T(128)} %bitcast.240, s32[]{:T(128)} %bitcast.241, s32[]{:T(128)} %bitcast.242, s32[]{:T(128)} %bitcast.243, s32[]{:T(128)} %bitcast.244, s32[]{:T(128)} %bitcast.245, ...), kind=kLoop, calls=%fused_computation.52.clone.1 | loop fusion | flops 71168 | bytes 2820 | tf_op jit(solution)/shard_map/while/body/eval_jaxpr/lt | solution.py:65
  727.7 5.7 bitcast_add_fusion.5
  737.5 40.6 %select_compare_fusion.2 = pred[512]{0:T(512)(128)(4,1)S(1)} fusion(s32[512]{0:T(512)S(1)} %bitcast.311, s32[]{:T(128)} %bitcast.237, s32[]{:T(128)} %bitcast.238, s32[]{:T(128)} %bitcast.239, s32[]{:T(128)} %bitcast.240, s32[]{:T(128)} %bitcast.241, s32[]{:T(128)} %bitcast.242, s32[]{:T(128)} %bitcast.243, s32[]{:T(128)} %bitcast.244, s32[]{:T(128)} %bitcast.245, ...), kind=kLoop, calls=%fused_computation.52.clone.1 | loop fusion | flops 71168 | bytes 2820 | tf_op jit(solution)/shard_map/while/body/eval_jaxpr/lt | solution.py:65
  791.7 5.7 bitcast_add_fusion.5
  801.5 40.6 %select_compare_fusion.2 = pred[512]{0:T(512)(128)(4,1)S(1)} fusion(s32[512]{0:T(512)S(1)} %bitcast.311, s32[]{:T(128)} %bitcast.237, s32[]{:T(128)} %bitcast.238, s32[]{:T(128)} %bitcast.239, s32[]{:T(128)} %bitcast.240, s32[]{:T(128)} %bitcast.241, s32[]{:T(128)} %bitcast.242, s32[]{:T(128)} %bitcast.243, s32[]{:T(128)} %bitcast.244, s32[]{:T(128)} %bitcast.245, ...), kind=kLoop, calls=%fused_computation.52.clone.1 | loop fusion | flops 71168 | bytes 2820 | tf_op jit(solution)/shard_map/while/body/eval_jaxpr/lt | solution.py:65
  855.7 5.7 bitcast_add_fusion.5
  865.5 40.6 %select_compare_fusion.2 = pred[512]{0:T(512)(128)(4,1)S(1)} fusion(s32[512]{0:T(512)S(1)} %bitcast.311, s32[]{:T(128)} %bitcast.237, s32[]{:T(128)} %bitcast.238, s32[]{:T(128)} %bitcast.239, s32[]{:T(128)} %bitcast.240, s32[]{:T(128)} %bitcast.241, s32[]{:T(128)} %bitcast.242, s32[]{:T(128)} %bitcast.243, s32[]{:T(128)} %bitcast.244, s32[]{:T(128)} %bitcast.245, ...), kind=kLoop, calls=%fused_computation.52.clone.1 | loop fusion | flops 71168 | bytes 2820 | tf_op jit(solution)/shard_map/while/body/eval_jaxpr/lt | solution.py:65
  919.7 5.7 bitcast_add_fusion.5
  929.6 40.6 %select_compare_fusion.2 = pred[512]{0:T(512)(128)(4,1)S(1)} fusion(s32[512]{0:T(512)S(1)} %bitcast.311, s32[]{:T(128)} %bitcast.237, s32[]{:T(128)} %bitcast.238, s32[]{:T(128)} %bitcast.239, s32[]{:T(128)} %bitcast.240, s32[]{:T(128)} %bitcast.241, s32[]{:T(128)} %bitcast.242, s32[]{:T(128)} %bitcast.243, s32[]{:T(128)} %bitcast.244, s32[]{:T(128)} %bitcast.245, ...), kind=kLoop, calls=%fused_computation.52.clone.1 | loop fusion | flops 71168 | bytes 2820 | tf_op jit(solution)/shard_map/while/body/eval_jaxpr/lt | solution.py:65
  983.8 5.7 bitcast_add_fusion.5
  993.6 40.6 %select_compare_fusion.2 = pred[512]{0:T(512)(128)(4,1)S(1)} fusion(s32[512]{0:T(512)S(1)} %bitcast.311, s32[]{:T(128)} %bitcast.237, s32[]{:T(128)} %bitcast.238, s32[]{:T(128)} %bitcast.239, s32[]{:T(128)} %bitcast.240, s32[]{:T(128)} %bitcast.241, s32[]{:T(128)} %bitcast.242, s32[]{:T(128)} %bitcast.243, s32[]{:T(128)} %bitcast.244, s32[]{:T(128)} %bitcast.245, ...), kind=kLoop, calls=%fused_computation.52.clone.1 | loop fusion | flops 71168 | bytes 2820 | tf_op jit(solution)/shard_map/while/body/eval_jaxpr/lt | solution.py:65
  1047.8 5.7 bitcast_add_fusion.5
  1057.6 40.6 %select_compare_fusion.2 = pred[512]{0:T(512)(128)(4,1)S(1)} fusion(s32[512]{0:T(512)S(1)} %bitcast.311, s32[]{:T(128)} %bitcast.237, s32[]{:T(128)} %bitcast.238, s32[]{:T(128)} %bitcast.239, s32[]{:T(128)} %bitcast.240, s32[]{:T(128)} %bitcast.241, s32[]{:T(128)} %bitcast.242, s32[]{:T(128)} %bitcast.243, s32[]{:T(128)} %bitcast.244, s32[]{:T(128)} %bitcast.245, ...), kind=kLoop, calls=%fused_computation.52.clone.1 | loop fusion | flops 71168 | bytes 2820 | tf_op jit(solution)/shard_map/while/body/eval_jaxpr/lt | solution.py:65
  1111.8 5.7 bitcast_add_fusion.5
  1121.7 40.6 %select_compare_fusion.2 = pred[512]{0:T(512)(128)(4,1)S(1)} fusion(s32[512]{0:T(512)S(1)} %bitcast.311, s32[]{:T(128)} %bitcast.237, s32[]{:T(128)} %bitcast.238, s32[]{:T(128)} %bitcast.239, s32[]{:T(128)} %bitcast.240, s32[]{:T(128)} %bitcast.241, s32[]{:T(128)} %bitcast.242, s32[]{:T(128)} %bitcast.243, s32[]{:T(128)} %bitcast.244, s32[]{:T(128)} %bitcast.245, ...), kind=kLoop, calls=%fused_computation.52.clone.1 | loop fusion | flops 71168 | bytes 2820 | tf_op jit(solution)/shard_map/while/body/eval_jaxpr/lt | solution.py:65
  1175.8 5.7 bitcast_add_fusion.5
  1185.7 40.6 %select_compare_fusion.2 = pred[512]{0:T(512)(128)(4,1)S(1)} fusion(s32[512]{0:T(512)S(1)} %bitcast.311, s32[]{:T(128)} %bitcast.237, s32[]{:T(128)} %bitcast.238, s32[]{:T(128)} %bitcast.239, s32[]{:T(128)} %bitcast.240, s32[]{:T(128)} %bitcast.241, s32[]{:T(128)} %bitcast.242, s32[]{:T(128)} %bitcast.243, s32[]{:T(128)} %bitcast.244, s32[]{:T(128)} %bitcast.245, ...), kind=kLoop, calls=%fused_computation.52.clone.1 | loop fusion | flops 71168 | bytes 2820 | tf_op jit(solution)/shard_map/while/body/eval_jaxpr/lt | solution.py:65
  1239.9 5.7 bitcast_add_fusion.5
  1249.7 40.6 %select_compare_fusion.2 = pred[512]{0:T(512)(128)(4,1)S(1)} fusion(s32[512]{0:T(512)S(1)} %bitcast.311, s32[]{:T(128)} %bitcast.237, s32[]{:T(128)} %bitcast.238, s32[]{:T(128)} %bitcast.239, s32[]{:T(128)} %bitcast.240, s32[]{:T(128)} %bitcast.241, s32[]{:T(128)} %bitcast.242, s32[]{:T(128)} %bitcast.243, s32[]{:T(128)} %bitcast.244, s32[]{:T(128)} %bitcast.245, ...), kind=kLoop, calls=%fused_computation.52.clone.1 | loop fusion | flops 71168 | bytes 2820 | tf_op jit(solution)/shard_map/while/body/eval_jaxpr/lt | solution.py:65
  1303.9 5.7 bitcast_add_fusion.5
  1313.7 40.6 %select_compare_fusion.2 = pred[512]{0:T(512)(128)(4,1)S(1)} fusion(s32[512]{0:T(512)S(1)} %bitcast.311, s32[]{:T(128)} %bitcast.237, s32[]{:T(128)} %bitcast.238, s32[]{:T(128)} %bitcast.239, s32[]{:T(128)} %bitcast.240, s32[]{:T(128)} %bitcast.241, s32[]{:T(128)} %bitcast.242, s32[]{:T(128)} %bitcast.243, s32[]{:T(128)} %bitcast.244, s32[]{:T(128)} %bitcast.245, ...), kind=kLoop, calls=%fused_computation.52.clone.1 | loop fusion | flops 71168 | bytes 2820 | tf_op jit(solution)/shard_map/while/body/eval_jaxpr/lt | solution.py:65
  1367.9 5.7 bitcast_add_fusion.5
  1377.8 40.6 %select_compare_fusion.2 = pred[512]{0:T(512)(128)(4,1)S(1)} fusion(s32[512]{0:T(512)S(1)} %bitcast.311, s32[]{:T(128)} %bitcast.237, s32[]{:T(128)} %bitcast.238, s32[]{:T(128)} %bitcast.239, s32[]{:T(128)} %bitcast.240, s32[]{:T(128)} %bitcast.241, s32[]{:T(128)} %bitcast.242, s32[]{:T(128)} %bitcast.243, s32[]{:T(128)} %bitcast.244, s32[]{:T(128)} %bitcast.245, ...), kind=kLoop, calls=%fused_computation.52.clone.1 | loop fusion | flops 71168 | bytes 2820 | tf_op jit(solution)/shard_map/while/body/eval_jaxpr/lt | solution.py:65
  1432.0 5.7 bitcast_add_fusion.5
  (578 shorter events, 537.6 us)
Async XLA Ops:
  6.5 21.0 %copy-start = (s32[64]{0:T(128)S(1)}, s32[64]{0:T(128)}, u32[]{:S(2)}) copy-start(s32[64]{0:T(128)} %param.15) | copy-start | bytes 772
  6.5 110.6 %all-gather.3.cloned.1.call-start = ((), (), s32[]{:S(2)}) async-start(), calls=%async_computation | async-start | bytes 17039360 | tf_op jit(solution)/shard_map/all_gather | solution.py:86
  7.3 405.8 %all-gather.5.cloned.1.call-start = ((), (), s32[]{:S(2)}) async-start(), calls=%async_computation.1 | async-start | bytes 17039360 | tf_op jit(solution)/shard_map/all_gather | solution.py:87
  465.8 2.9 copy-start.1
  465.8 4.7 copy-start.2
  529.8 2.9 copy-start.1
  529.8 4.7 copy-start.2
  593.8 2.9 copy-start.1
  593.8 4.7 copy-start.2
  657.9 2.9 copy-start.1
  657.9 4.7 copy-start.2
  721.9 2.9 copy-start.1
  721.9 4.7 copy-start.2
  785.9 2.9 copy-start.1
  785.9 4.7 copy-start.2
  849.9 2.9 copy-start.1
  849.9 4.7 copy-start.2
  914.0 2.9 copy-start.1
  914.0 4.7 copy-start.2
  978.0 2.9 copy-start.1
  978.0 4.7 copy-start.2
  1042.0 2.9 copy-start.1
  1042.0 4.7 copy-start.2
  1106.0 2.9 copy-start.1
  1106.1 4.7 copy-start.2
  1170.1 2.9 copy-start.1
  1170.1 4.7 copy-start.2
  1234.1 2.9 copy-start.1
  1234.1 4.7 copy-start.2
  1298.1 2.9 copy-start.1
  1298.1 4.7 copy-start.2
  1362.2 2.9 copy-start.1
  1362.2 4.7 copy-start.2
  1426.2 2.9 copy-start.1
  1426.2 4.7 copy-start.2
Sparse Core Ops, SparseCore 0:
  10.3 106.8 all-gather.2
  120.0 103.9 all-gather.4
where the time goes:
time: 1460 us; the launch traced here: 1450 us
  other arithmetic  788 us (54%)
  local copies, waits for them, and re-layouts  290 us (20%)
  matrix products  261 us (18%)
  waiting for transfers between devices  89.8 us (6%)
    lt x16, other arithmetic, tree_seen(): linked = linked & (key_pos < key_count)[None, :]  650 us
    dot_general x32, matrix products, attend_piece(): jnp.einsum('rkgn,nkd->rkgd', expo.astype(jnp.bfloat16), current_values, p...  174 us
    while x160, local copies, waits for them, and re-layouts  123 us
    reduce_sum x32, other arithmetic, attend_piece(): total = total * factor + jnp.sum(expo, axis=-1)  98.7 us
    all_gather x1, waiting for transfers between devices, shards(): lax.all_gather(prompt_key_value, 'leaf', axis=1, tiled=True)  88.4 us
    dot_general x32, matrix products, attend_piece(): jnp.einsum('rkgd,nkd->rkgn', query_head_rows, current_keys, preferred_ele...  87.4 us
    slice x32, local copies, waits for them, and re-layouts, attend_piece(): block_portion[1].reshape(token_length, KEY_VALUE_HEADS, HEAD_SIZE)  72.3 us
    gather x64, local copies, waits for them, and re-layouts, tree_seen(): key_count = counts[key_block]  45.9 us
  transfers between devices with their start and end apart: 2, of which 1 were waited for; matrix products, arithmetic and copies ran while one was open for 22% of the time, Pallas kernels for 0%

commit v1 on v0

v1 whole, which is shorter than its diff:
```python
import functools
import math

import jax
import jax.numpy as jnp
from jax import lax
from jax.experimental import pallas as pl
from jax.experimental.pallas import tpu as pltpu
from jax.sharding import PartitionSpec as P

QUERY_HEADS = 28
KV_HEADS = 4
HEAD = 128
BLOCK = 128
LINE = 4
GROUP = QUERY_HEADS // KV_HEADS
WIDTH = GROUP * HEAD
ROWS = GROUP * BLOCK
RING = 16
HALF = RING // 2
OWN = LINE * BLOCK
PART = OWN // 2
STEP = 4 * PART
PROMPT = RING * OWN
TO_EXP2 = HEAD**-0.5 * math.log2(math.e)
LOWEST = -1e30
MESH = pl.DeviceIdType.MESH

SEM_PROMPT, SEM_TREE, SEM_QUERY, SEM_OUT, SEM_RING = 0, 4, 8, 12, 16
SEMS = SEM_RING + 4 * HALF


def shift_of(slot):
    return slot + slot // 2 - 2 * (slot // 3)


def kernel(queries, branch, prompt, parents, counts, out, q_buf, kv, tree, top, total, acc, stage, send_sem, recv_sem, local_sem):
    leaf = lax.axis_index("leaf")
    x = lax.rem(leaf, LINE)
    line = leaf - x
    y = lax.rem(leaf // LINE, LINE)
    z = leaf // (LINE * LINE)

    def ring_places(outer, inner):
        place = LINE * outer + lax.rem(inner + outer, LINE)
        found = []
        for turn in (1, RING - 1):
            there = lax.rem(place + turn, RING)
            far = there // LINE
            found.append((far, lax.rem(lax.rem(there, LINE) + 3 * far, LINE)))
        return found

    ring_devices = [[(a * LINE + b) * LINE + x for a, b in ring_places(z, y)],
                    [(b * LINE + a) * LINE + x for a, b in ring_places(y, z)]]
    line_devices = [line + lax.rem(x + d, LINE) for d in range(1, LINE)]

    barrier = pltpu.get_barrier_semaphore()
    partners = line_devices + ring_devices[0] + ring_devices[1]
    for device in partners:
        pl.semaphore_signal(barrier, inc=1, device_id={"leaf": device}, device_id_type=MESH)

    def columns(place, width):
        return pl.ds(pl.multiple_of(place * width, width), width)

    own_prompt = pltpu.make_async_copy(prompt.at[:, :, columns(x, HEAD)], kv.at[:, pl.ds(0, BLOCK), :], local_sem.at[0])
    own_query = pltpu.make_async_copy(queries.at[:, columns(x, WIDTH)], q_buf.at[0], local_sem.at[1])
    own_tree = pltpu.make_async_copy(branch.at[:, :, columns(x, HEAD)], tree.at[:, pl.ds(0, BLOCK), :], local_sem.at[2])
    own_out = pltpu.make_async_copy(stage.at[0], out.at[:, columns(x, WIDTH)], local_sem.at[3])
    own_prompt.start()
    own_query.start()
    own_tree.start()
    pl.semaphore_wait(barrier, len(partners))

    def to_line(slot, source, target, first):
        there = lax.rem(x + shift_of(slot), LINE)
        return pltpu.make_async_remote_copy(
            src_ref=source(there), dst_ref=target, send_sem=send_sem.at[first + slot], recv_sem=recv_sem.at[first + slot],
            device_id={"leaf": line + there}, device_id_type=MESH)

    def prompt_copy(slot):
        return to_line(slot, lambda there: prompt.at[:, :, columns(there, HEAD)], kv.at[:, pl.ds(slot * BLOCK, BLOCK), :], SEM_PROMPT)

    def tree_copy(slot):
        return to_line(slot, lambda there: branch.at[:, :, columns(there, HEAD)], tree.at[:, pl.ds(slot * BLOCK, BLOCK), :], SEM_TREE)

    def query_copy(slot):
        return to_line(slot, lambda there: queries.at[:, columns(there, WIDTH)], q_buf.at[slot], SEM_QUERY)

    def out_copy(slot):
        there = lax.rem(x - shift_of(slot) + LINE, LINE)
        return pltpu.make_async_remote_copy(
            src_ref=stage.at[slot], dst_ref=out.at[:, columns(x, WIDTH)], send_sem=send_sem.at[SEM_OUT + slot],
            recv_sem=recv_sem.at[SEM_OUT + slot], device_id={"leaf": line + there}, device_id_type=MESH)

    def region(step, stream):
        if step == 0:
            return pl.ds(stream // 2 * PART, PART)
        if step < HALF:
            return pl.ds(OWN + (step - 1) * STEP + stream * PART, PART)
        return pl.ds(OWN + (HALF - 1) * STEP + stream * (PART // 2), PART // 2)

    def ring_copy(step, stream):
        source = region(step - 1, stream)
        if step == HALF:
            source = pl.ds(source.start + stream % 2 * (PART // 2), PART // 2)
        sem = SEM_RING + (step - 1) * 4 + stream
        return pltpu.make_async_remote_copy(
            src_ref=kv.at[:, source, :], dst_ref=kv.at[:, region(step, stream), :], send_sem=send_sem.at[sem],
            recv_sem=recv_sem.at[sem], device_id={"leaf": ring_devices[stream // 2][stream % 2]}, device_id_type=MESH)

    def advance(step):
        for stream in range(4):
            if step:
                ring_copy(step, stream).wait_recv()
            if step < HALF:
                ring_copy(step + 1, stream).start()

    for slot in (1, 2, 3):
        prompt_copy(slot).start()
    for slot in (1, 2):
        query_copy(slot).start()
    for slot in (1, 2, 3):
        tree_copy(slot).start()
    query_copy(3).start()

    parent = [parents[line + i] - line for i in range(LINE)]
    above = {}
    for b in range(1, LINE):
        for c in range(b):
            seen = jnp.where(parent[b] == c, 1, 0)
            for mid in range(c + 1, b):
                seen = jnp.maximum(seen, jnp.where(parent[b] == mid, above[mid, c], 0))
            above[b, c] = seen

    def masked(scores, slot):
        mine = lax.rem(x - shift_of(slot) + LINE, LINE)
        row = lax.broadcasted_iota(jnp.int32, (BLOCK, BLOCK), 0)
        column = lax.broadcasted_iota(jnp.int32, (BLOCK, BLOCK), 1)
        heads = [[] for _ in range(GROUP)]
        for other in range(LINE):
            block = lax.rem(x - shift_of(other) + LINE, LINE)
            linked = jnp.int32(0)
            for (b, c), seen in above.items():
                linked = jnp.where((mine == b) & (block == c), seen, linked)
            limit = linked * counts[line + block]
            limits = jnp.where(mine == block, row + 1, limit)
            for g in range(GROUP):
                piece = scores[g * BLOCK:(g + 1) * BLOCK, other * BLOCK:(other + 1) * BLOCK]
                heads[g].append(jnp.where(column < limits, piece, LOWEST))
        return jnp.concatenate([jnp.concatenate(head, axis=1) for head in heads], axis=0)

    def score(q, keys):
        return lax.dot_general(q, keys, (((1,), (1,)), ((), ())), preferred_element_type=jnp.float32)

    def attend(slot, chunks, first=False, last=False):
        q = jnp.concatenate([q_buf[slot, :, g * HEAD:(g + 1) * HEAD] for g in range(GROUP)], axis=0)
        if first:
            m, l, a = jnp.full((ROWS, HEAD), LOWEST, jnp.float32), jnp.zeros((ROWS, HEAD), jnp.float32), jnp.zeros((ROWS, HEAD), jnp.float32)
        else:
            m, l, a = top[slot], total[slot], acc[slot]

        def scores_of(chunk):
            buffer, start, length = chunk
            s = score(q, buffer[0, pl.ds(start, length), :])
            return masked(s, slot) if buffer is tree else s

        s = scores_of(chunks[0])
        for n, (buffer, start, length) in enumerate(chunks):
            following = scores_of(chunks[n + 1]) if n + 1 < len(chunks) else None
            new = jnp.maximum(m, jnp.broadcast_to(jnp.max(s, axis=1, keepdims=True), (ROWS, HEAD)))
            factor = jnp.exp2((m - new) * TO_EXP2)
            weights = jnp.concatenate(
                [jnp.exp2((s[:, i:i + HEAD] - new) * TO_EXP2).astype(jnp.bfloat16) for i in range(0, length, HEAD)], axis=1)
            values = buffer[1, pl.ds(start, length), :]
            both = jnp.dot(weights, jnp.concatenate([values, jnp.ones_like(values)], axis=1), preferred_element_type=jnp.float32)
            a = a * factor + both[:, :HEAD]
            l = l * factor + both[:, HEAD:]
            m, s = new, following
        if not last:
            top[slot], total[slot], acc[slot] = m, l, a
            return
        mine = lax.rem(x - shift_of(slot) + LINE, LINE)
        live = lax.broadcasted_iota(jnp.int32, (BLOCK, HEAD), 0) < counts[line + mine]
        for g in range(GROUP):
            rows = slice(g * BLOCK, (g + 1) * BLOCK)
            stage[slot, :, g * HEAD:(g + 1) * HEAD] = jnp.where(live, a[rows] / l[rows], 0.0).astype(stage.dtype)

    def ring_chunks(steps, length):
        start, end = OWN + (steps[0] - 1) * STEP, min(OWN + steps[-1] * STEP, PROMPT)
        return [(kv, at, min(length, end - at)) for at in range(start, end, length)]

    beginning = [(kv, 0, OWN), (tree, 0, OWN)]

    own_prompt.wait()
    for slot in (1, 2, 3):
        prompt_copy(slot).wait_recv()
    advance(0)
    own_query.wait()
    own_tree.wait()
    for slot in (1, 2, 3):
        tree_copy(slot).wait_recv()
    attend(0, beginning, first=True)
    advance(1)
    for slot in (1, 2):
        query_copy(slot).wait_recv()

    def two(i, c):
        attend(i + 1, beginning + ring_chunks((1,), 1024), first=True)
        return c

    lax.fori_loop(0, 2, two, 0)
    attend(0, ring_chunks((1,), 512))
    advance(2)

    def three(i, c):
        attend(i, ring_chunks((2,), 512))
        return c

    lax.fori_loop(0, 3, three, 0)
    advance(3)
    query_copy(3).wait_recv()
    attend(3, beginning + ring_chunks((1, 2), 1024), first=True)
    advance(4)

    def four(i, c):
        attend(i, ring_chunks((3, 4), 1024))

        @pl.when(i == 1)
        def _():
            advance(5)

        @pl.when(i == 2)
        def _():
            advance(6)

        return c

    lax.fori_loop(0, 4, four, 0)
    advance(7)
    advance(8)

    def final(i, c):
        slot = 3 - i
        attend(slot, ring_chunks((5, 6, 7, 8), 1024), last=True)

        @pl.when(i < 3)
        def _():
            out_copy(slot).start()

        return c

    lax.fori_loop(0, 4, final, 0)
    own_out.start()
    for slot in (1, 2, 3):
        prompt_copy(slot).wait_send()
        tree_copy(slot).wait_send()
        query_copy(slot).wait_send()
        out_copy(slot).wait_send()
    for step in range(1, HALF + 1):
        for stream in range(4):
            ring_copy(step, stream).wait_send()
    for slot in (1, 2, 3):
        out_copy(slot).wait_recv()
    own_out.wait()


def shards(queries, branch, prompt, parents, counts):
    return pl.pallas_call(
        kernel,
        out_shape=jax.ShapeDtypeStruct(queries.shape, queries.dtype),
        in_specs=[pl.BlockSpec(memory_space=pl.ANY)] * 3 + [pl.BlockSpec(memory_space=pltpu.SMEM)] * 2,
        out_specs=pl.BlockSpec(memory_space=pl.ANY),
        scratch_shapes=[
            pltpu.VMEM((LINE, BLOCK, WIDTH), jnp.bfloat16),
            pltpu.VMEM((2, PROMPT, HEAD), jnp.bfloat16),
            pltpu.VMEM((2, OWN, HEAD), jnp.bfloat16),
            pltpu.VMEM((LINE, ROWS, HEAD), jnp.float32),
            pltpu.VMEM((LINE, ROWS, HEAD), jnp.float32),
            pltpu.VMEM((LINE, ROWS, HEAD), jnp.float32),
            pltpu.VMEM((LINE, BLOCK, WIDTH), jnp.bfloat16),
            pltpu.SemaphoreType.DMA((SEMS,)),
            pltpu.SemaphoreType.DMA((SEMS,)),
            pltpu.SemaphoreType.DMA((4,)),
        ],
        compiler_params=pltpu.CompilerParams(
            collective_id=0, has_side_effects=True, vmem_limit_bytes=52 * 2**20
        ),
    )(queries, branch, prompt, parents, counts)


def solution(mesh):
    placed = (
        P(("rep", "leaf"), None),
        P(None, ("rep", "leaf"), None),
        P(None, ("rep", "leaf"), None),
        P("rep"),
        P("rep"),
    )
    return jax.shard_map(
        shards, mesh=mesh, in_specs=placed, out_specs=P(("rep", "leaf"), None), check_vma=False
    )
```

time: 1460 us -> 81 us (0.06)
  other arithmetic: 788 us -> 0 us
  local copies, waits for them, and re-layouts: 290 us -> 4.13 us
  matrix products: 261 us -> 0 us
  waiting for transfers between devices: 89.8 us -> 0 us
  Pallas kernels: 0 us -> 76.7 us
    lt x17 -> x0, other arithmetic: 650 us -> none  [the longest x16 650 us: tree_seen(): linked = linked & (key_pos < key_count)[None, :]]
    dot_general x64 -> x0, matrix products: 261 us -> none  [the longest x32 174 us: attend_piece(): jnp.einsum('rkgn,nkd->rkgd', expo.astype(jnp.bfloat16), current_values, p...]
    while x160 -> x0, local copies, waits for them, and re-layouts: 123 us -> none
    reduce_sum x32 -> x0, other arithmetic: 98.7 us -> none  [attend_piece(): total = total * factor + jnp.sum(expo, axis=-1)]
    all_gather x2 -> x0, waiting for transfers between devices: 88.4 us -> none  [the longest x1 88.4 us: shards(): lax.all_gather(prompt_key_value, 'leaf', axis=1, tiled=True)]
    gather x90 -> x0, local copies, waits for them, and re-layouts: 80.3 us -> none  [the longest x64 45.9 us: tree_seen(): key_count = counts[key_block]]
    pallas_call x0 -> x1, Pallas kernels: none -> 76.7 us  [shards(): pl.pallas_call(kernel, out_shape=jax.ShapeDtypeStruct(queries.shape, quer...]
    slice x32 -> x0, local copies, waits for them, and re-layouts: 72.3 us -> none  [attend_piece(): block_portion[1].reshape(token_length, KEY_VALUE_HEADS, HEAD_SIZE)]
  transfers between devices with their start and end apart: 2 -> 0, of which waited for: 1 -> 0; matrix products, arithmetic and copies ran while one was open for 22% -> 0% of each run, Pallas kernels for 0% -> 0%
where the time goes in v1:
time: 81 us; the launch traced here: 80.8 us
  Pallas kernels  76.7 us (95%)
  local copies, waits for them, and re-layouts  4.13 us (5%)
    pallas_call x1, Pallas kernels, shards(): pl.pallas_call(kernel, out_shape=jax.ShapeDtypeStruct(queries.shape, quer...  76.7 us
    unnamed x9, local copies, waits for them, and re-layouts  4.13 us

profile of v1, /device:TPU:0, one launch (start us, length us, event | category | flops | bytes accessed | tf_op | source)
XLA Modules:
  0.0 80.8 jit_solution(8877723807203883762)
XLA Ops:
  0.0 0.0 copy-start
  0.0 0.9 %copy-done = bf16[2,128,512]{2,1,0:T(8,128)(2,1)S(1)} copy-done((bf16[2,128,512]{2,1,0:T(8,128)(2,1)S(1)}, bf16[2,128,512]{2,1,0:T(8,128)(2,1)}, u32[]{:S(2)}) %copy-start) | copy-done | bytes 262168
  1.0 0.0 copy-start.1
  1.0 0.9 %copy-done.1 = bf16[2,128,512]{2,1,0:T(8,128)(2,1)S(1)} copy-done((bf16[2,128,512]{2,1,0:T(8,128)(2,1)S(1)}, bf16[2,128,512]{2,1,0:T(8,128)(2,1)}, u32[]{:S(2)}) %copy-start.1) | copy-done | bytes 262168
  1.9 0.0 copy-start.2
  1.9 0.7 copy-done.2
  2.6 0.0 copy-start.3
  2.6 0.7 copy-done.3
  3.2 76.7 %shard_map.55 = bf16[128,3584]{1,0:T(8,128)(2,1)S(1)} custom-call(bf16[128,3584]{1,0:T(8,128)(2,1)} %queries.1, bf16[2,128,512]{2,1,0:T(8,128)(2,1)S(1)} %copy-done, bf16[2,128,512]{2,1,0:T(8,128)(2,1)S(1)} %copy-done.1, s32[64]{0:T(128)S(1)} %copy-done.2, s32[64]{0:T(128)S(1)} %copy-done.3), custom_call_target="tpu_custom_call" | custom-call | tf_op jit(solution)/shard_map/pallas_call | solution.py:268
  79.9 0.9 %copy.7 = bf16[128,3584]{1,0:T(8,128)(2,1)} copy(bf16[128,3584]{1,0:T(8,128)(2,1)S(1)} %shard_map.55) | data formatting | bytes 1835008
Async XLA Ops:
  0.0 0.9 %copy-start = (bf16[2,128,512]{2,1,0:T(8,128)(2,1)S(1)}, bf16[2,128,512]{2,1,0:T(8,128)(2,1)}, u32[]{:S(2)}) copy-start(bf16[2,128,512]{2,1,0:T(8,128)(2,1)} %branch.1) | copy-start | bytes 786436
  1.0 0.9 %copy-start.1 = (bf16[2,128,512]{2,1,0:T(8,128)(2,1)S(1)}, bf16[2,128,512]{2,1,0:T(8,128)(2,1)}, u32[]{:S(2)}) copy-start(bf16[2,128,512]{2,1,0:T(8,128)(2,1)} %prompt.1) | copy-start | bytes 786436
  1.9 0.7 copy-start.2
  2.6 0.7 copy-start.3

commit v2 on v1

--- a/solution.py
+++ b/solution.py
@@ -16,59 +16,62 @@
 GROUP = QUERY_HEADS // KV_HEADS
 WIDTH = GROUP * HEAD
 ROWS = GROUP * BLOCK
-RING = 16
-HALF = RING // 2
-OWN = LINE * BLOCK
-PART = OWN // 2
-STEP = 4 * PART
-PROMPT = RING * OWN
+PLANE = 16
+PEERS = 6
+RELAYS = 18
+PROMPT = PLANE * LINE * BLOCK
+REST = (LINE - 1) * BLOCK
+AT_PEERS = BLOCK
+AT_REST = AT_PEERS + PEERS * BLOCK
+AT_RELAYS = AT_REST + REST
+AT_REST_PEERS = AT_RELAYS + RELAYS * BLOCK // 2
+AT_REST_RELAYS = AT_REST_PEERS + PEERS * REST
 TO_EXP2 = HEAD**-0.5 * math.log2(math.e)
 LOWEST = -1e30
 MESH = pl.DeviceIdType.MESH
 
-SEM_PROMPT, SEM_TREE, SEM_QUERY, SEM_OUT, SEM_RING = 0, 4, 8, 12, 16
-SEMS = SEM_RING + 4 * HALF
+SEM_PROMPT, SEM_TREE, SEM_QUERY, SEM_OUT, SEM_PEERS, SEM_REST_PEERS = 0, 4, 8, 12, 16, 22
+SEM_RELAYS, SEM_REST_RELAYS, SEMS = 28, 46, 64
 
 
 def shift_of(slot):
     return slot + slot // 2 - 2 * (slot // 3)
 
 
-def kernel(queries, branch, prompt, parents, counts, out, q_buf, kv, tree, top, total, acc, stage, send_sem, recv_sem, local_sem):
+def kernel(queries, branch, prompt, parents_in, counts_in, out, q_buf, kv, tree, top, total, acc, stage, prompt_in, parents, counts,
+           send_sem, recv_sem, local_sem):
     leaf = lax.axis_index("leaf")
     x = lax.rem(leaf, LINE)
     line = leaf - x
     y = lax.rem(leaf // LINE, LINE)
     z = leaf // (LINE * LINE)
 
-    def ring_places(outer, inner):
-        place = LINE * outer + lax.rem(inner + outer, LINE)
-        found = []
-        for turn in (1, RING - 1):
-            there = lax.rem(place + turn, RING)
-            far = there // LINE
-            found.append((far, lax.rem(lax.rem(there, LINE) + 3 * far, LINE)))
-        return found
-
-    ring_devices = [[(a * LINE + b) * LINE + x for a, b in ring_places(z, y)],
-                    [(b * LINE + a) * LINE + x for a, b in ring_places(y, z)]]
+    peers = [(z * LINE + lax.rem(y + d, LINE)) * LINE + x for d in (1, 3, 2)]
+    peers += [(lax.rem(z + d, LINE) * LINE + y) * LINE + x for d in (1, 3, 2)]
     line_devices = [line + lax.rem(x + d, LINE) for d in range(1, LINE)]
 
     barrier = pltpu.get_barrier_semaphore()
-    partners = line_devices + ring_devices[0] + ring_devices[1]
+    partners = line_devices + peers
     for device in partners:
         pl.semaphore_signal(barrier, inc=1, device_id={"leaf": device}, device_id_type=MESH)
 
     def columns(place, width):
         return pl.ds(pl.multiple_of(place * width, width), width)
 
+    whole_prompt = pltpu.make_async_copy(prompt, prompt_in, local_sem.at[4])
     own_prompt = pltpu.make_async_copy(prompt.at[:, :, columns(x, HEAD)], kv.at[:, pl.ds(0, BLOCK), :], local_sem.at[0])
+    small = [pltpu.make_async_copy(parents_in, parents, local_sem.at[5]), pltpu.make_async_copy(counts_in, counts, local_sem.at[6])]
     own_query = pltpu.make_async_copy(queries.at[:, columns(x, WIDTH)], q_buf.at[0], local_sem.at[1])
     own_tree = pltpu.make_async_copy(branch.at[:, :, columns(x, HEAD)], tree.at[:, pl.ds(0, BLOCK), :], local_sem.at[2])
     own_out = pltpu.make_async_copy(stage.at[0], out.at[:, columns(x, WIDTH)], local_sem.at[3])
     own_prompt.start()
     own_query.start()
     own_tree.start()
+    whole_prompt.start()
+    for copy in small:
+        copy.start()
+    own_prompt.wait()
+    whole_prompt.wait()
     pl.semaphore_wait(barrier, len(partners))
 
     def to_line(slot, source, target, first):
@@ -78,7 +81,7 @@
             device_id={"leaf": line + there}, device_id_type=MESH)
 
     def prompt_copy(slot):
-        return to_line(slot, lambda there: prompt.at[:, :, columns(there, HEAD)], kv.at[:, pl.ds(slot * BLOCK, BLOCK), :], SEM_PROMPT)
+        return to_line(slot, lambda there: prompt_in.at[:, :, columns(there, HEAD)], kv.at[:, pl.ds(AT_REST + (slot - 1) * BLOCK, BLOCK), :], SEM_PROMPT)
 
     def tree_copy(slot):
         return to_line(slot, lambda there: branch.at[:, :, columns(there, HEAD)], tree.at[:, pl.ds(slot * BLOCK, BLOCK), :], SEM_TREE)
@@ -92,36 +95,41 @@
             src_ref=stage.at[slot], dst_ref=out.at[:, columns(x, WIDTH)], send_sem=send_sem.at[SEM_OUT + slot],
             recv_sem=recv_sem.at[SEM_OUT + slot], device_id={"leaf": line + there}, device_id_type=MESH)
 
-    def region(step, stream):
-        if step == 0:
-            return pl.ds(stream // 2 * PART, PART)
-        if step < HALF:
-            return pl.ds(OWN + (step - 1) * STEP + stream * PART, PART)
-        return pl.ds(OWN + (HALF - 1) * STEP + stream * (PART // 2), PART // 2)
-
-    def ring_copy(step, stream):
-        source = region(step - 1, stream)
-        if step == HALF:
-            source = pl.ds(source.start + stream % 2 * (PART // 2), PART // 2)
-        sem = SEM_RING + (step - 1) * 4 + stream
+    def peer_copy(rest, peer):
+        start, length = (AT_REST, REST) if rest else (0, BLOCK)
+        to = (AT_REST_PEERS if rest else AT_PEERS) + peer * length
+        sem = (SEM_REST_PEERS if rest else SEM_PEERS) + peer
         return pltpu.make_async_remote_copy(
-            src_ref=kv.at[:, source, :], dst_ref=kv.at[:, region(step, stream), :], send_sem=send_sem.at[sem],
-            recv_sem=recv_sem.at[sem], device_id={"leaf": ring_devices[stream // 2][stream % 2]}, device_id_type=MESH)
-
-    def advance(step):
-        for stream in range(4):
-            if step:
-                ring_copy(step, stream).wait_recv()
-            if step < HALF:
-                ring_copy(step + 1, stream).start()
-
-    for slot in (1, 2, 3):
+            src_ref=kv.at[:, pl.ds(start, length), :], dst_ref=kv.at[:, pl.ds(to, length), :], send_sem=send_sem.at[sem],
+            recv_sem=recv_sem.at[sem], device_id={"leaf": peers[peer]}, device_id_type=MESH)
+
+    def relay_copy(rest, peer, turn):
+        half = (REST if rest else BLOCK) // 2
+        start = (AT_REST_PEERS if rest else AT_PEERS) + (2 * peer + peer // 3) * half
+        index = 3 * peer + turn
+        sem = (SEM_REST_RELAYS if rest else SEM_RELAYS) + index
+        to = (AT_REST_RELAYS if rest else AT_RELAYS) + index * half
+        return pltpu.make_async_remote_copy(
+            src_ref=kv.at[:, pl.ds(start, half), :], dst_ref=kv.at[:, pl.ds(to, half), :], send_sem=send_sem.at[sem],
+            recv_sem=recv_sem.at[sem], device_id={"leaf": peers[3 - peer // 3 * 3 + turn]}, device_id_type=MESH)
+
+    NEAR, FAR = (0, 3, 1, 4), (2, 5)
+
+    def relay(rest, which):
+        for peer in which:
+            peer_copy(rest, peer).wait_recv()
+            for turn in range(3):
+                relay_copy(rest, peer, turn).start()
+
+    for slot in (1, 2):
         prompt_copy(slot).start()
+    for peer in NEAR + FAR:
+        peer_copy(0, peer).start()
+    prompt_copy(3).start()
     for slot in (1, 2):
         query_copy(slot).start()
-    for slot in (1, 2, 3):
-        tree_copy(slot).start()
-    query_copy(3).start()
+    for copy in small:
+        copy.wait()
 
     parent = [parents[line + i] - line for i in range(LINE)]
     above = {}
@@ -185,63 +193,70 @@
             rows = slice(g * BLOCK, (g + 1) * BLOCK)
             stage[slot, :, g * HEAD:(g + 1) * HEAD] = jnp.where(live, a[rows] / l[rows], 0.0).astype(stage.dtype)
 
-    def ring_chunks(steps, length):
-        start, end = OWN + (steps[0] - 1) * STEP, min(OWN + steps[-1] * STEP, PROMPT)
-        return [(kv, at, min(length, end - at)) for at in range(start, end, length)]
-
-    beginning = [(kv, 0, OWN), (tree, 0, OWN)]
-
-    own_prompt.wait()
+    def chunks(*lengths):
+        start, found = lengths[0], []
+        for length in lengths[1:]:
+            found.append((kv, start, length))
+            start += length
+        return found
+
+    first = chunks(0, 768)
+    second = chunks(768, 768, 768) + [(tree, 0, LINE * BLOCK)]
+    third = chunks(2304, 768, 768, 768)
+    fourth = chunks(4608, 1024, 1024, 1024, 512)
+
+    relay(0, NEAR)
+    relay(0, FAR)
+    query_copy(3).start()
+    for slot in (1, 2, 3):
+        tree_copy(slot).start()
+    own_query.wait()
+    attend(0, first, first=True)
     for slot in (1, 2, 3):
         prompt_copy(slot).wait_recv()
-    advance(0)
-    own_query.wait()
-    own_tree.wait()
-    for slot in (1, 2, 3):
-        tree_copy(slot).wait_recv()
-    attend(0, beginning, first=True)
-    advance(1)
+    for peer in NEAR + FAR:
+        peer_copy(1, peer).start()
     for slot in (1, 2):
         query_copy(slot).wait_recv()
 
-    def two(i, c):
-        attend(i + 1, beginning + ring_chunks((1,), 1024), first=True)
+    def near_first(i, c):
+        attend(i + 1, first, first=True)
         return c
 
-    lax.fori_loop(0, 2, two, 0)
-    attend(0, ring_chunks((1,), 512))
-    advance(2)
-
-    def three(i, c):
-        attend(i, ring_chunks((2,), 512))
-        return c
-
-    lax.fori_loop(0, 3, three, 0)
-    advance(3)
-    query_copy(3).wait_recv()
-    attend(3, beginning + ring_chunks((1, 2), 1024), first=True)
-    advance(4)
-
-    def four(i, c):
-        attend(i, ring_chunks((3, 4), 1024))
+    lax.fori_loop(0, 2, near_first, 0)
+    for peer in range(PEERS):
+        for turn in range(3):
+            relay_copy(0, peer, turn).wait_recv()
+    own_tree.wait()
+    for slot in (1, 2, 3):
+        tree_copy(slot).wait_recv()
+
+    def near_second(i, c):
+        attend(i, second)
 
         @pl.when(i == 1)
         def _():
-            advance(5)
-
-        @pl.when(i == 2)
-        def _():
-            advance(6)
+            relay(1, NEAR)
 
         return c
 
-    lax.fori_loop(0, 4, four, 0)
-    advance(7)
-    advance(8)
+    lax.fori_loop(0, 3, near_second, 0)
+    query_copy(3).wait_recv()
+    attend(3, first + second, first=True)
+    relay(1, FAR)
+
+    def all_third(i, c):
+        attend(i, third)
+        return c
+
+    lax.fori_loop(0, LINE, all_third, 0)
+    for peer in range(PEERS):
+        for turn in range(3):
+            relay_copy(1, peer, turn).wait_recv()
 
     def final(i, c):
         slot = 3 - i
-        attend(slot, ring_chunks((5, 6, 7, 8), 1024), last=True)
+        attend(slot, fourth, last=True)
 
         @pl.when(i < 3)
         def _():
@@ -256,9 +271,11 @@
         tree_copy(slot).wait_send()
         query_copy(slot).wait_send()
         out_copy(slot).wait_send()
-    for step in range(1, HALF + 1):
-        for stream in range(4):
-            ring_copy(step, stream).wait_send()
+    for rest in range(2):
+        for peer in range(PEERS):
+            peer_copy(rest, peer).wait_send()
+            for turn in range(3):
+                relay_copy(rest, peer, turn).wait_send()
     for slot in (1, 2, 3):
         out_copy(slot).wait_recv()
     own_out.wait()
@@ -268,19 +285,22 @@
     return pl.pallas_call(
         kernel,
         out_shape=jax.ShapeDtypeStruct(queries.shape, queries.dtype),
-        in_specs=[pl.BlockSpec(memory_space=pl.ANY)] * 3 + [pl.BlockSpec(memory_space=pltpu.SMEM)] * 2,
-        out_specs=pl.BlockSpec(memory_space=pl.ANY),
+        in_specs=[pl.BlockSpec(memory_space=pltpu.HBM)] * 5,
+        out_specs=pl.BlockSpec(memory_space=pltpu.HBM),
         scratch_shapes=[
             pltpu.VMEM((LINE, BLOCK, WIDTH), jnp.bfloat16),
             pltpu.VMEM((2, PROMPT, HEAD), jnp.bfloat16),
-            pltpu.VMEM((2, OWN, HEAD), jnp.bfloat16),
+            pltpu.VMEM((2, LINE * BLOCK, HEAD), jnp.bfloat16),
             pltpu.VMEM((LINE, ROWS, HEAD), jnp.float32),
             pltpu.VMEM((LINE, ROWS, HEAD), jnp.float32),
             pltpu.VMEM((LINE, ROWS, HEAD), jnp.float32),
             pltpu.VMEM((LINE, BLOCK, WIDTH), jnp.bfloat16),
+            pltpu.VMEM((2, BLOCK, KV_HEADS * HEAD), jnp.bfloat16),
+            pltpu.SMEM((64,), jnp.int32),
+            pltpu.SMEM((64,), jnp.int32),
             pltpu.SemaphoreType.DMA((SEMS,)),
             pltpu.SemaphoreType.DMA((SEMS,)),
-            pltpu.SemaphoreType.DMA((4,)),
+            pltpu.SemaphoreType.DMA((7,)),
         ],
         compiler_params=pltpu.CompilerParams(
             collective_id=0, has_side_effects=True, vmem_limit_bytes=52 * 2**20

time: 81 us -> 67.3 us (0.83)
  Pallas kernels: 76.7 us -> 63 us
    pallas_call x1, Pallas kernels: 76.7 us -> 63 us  [shards(): pl.pallas_call(kernel, out_shape=jax.ShapeDtypeStruct(queries.shape, quer...]
where the time goes in v2:
time: 67.3 us; the launch traced here: 67.2 us
  Pallas kernels  63 us (94%)
  local copies, waits for them, and re-layouts  4.13 us (6%)
    pallas_call x1, Pallas kernels, shards(): pl.pallas_call(kernel, out_shape=jax.ShapeDtypeStruct(queries.shape, quer...  63 us
    unnamed x9, local copies, waits for them, and re-layouts  4.13 us

profile of v2, /device:TPU:0, one launch (start us, length us, event | category | flops | bytes accessed | tf_op | source)
XLA Modules:
  0.0 67.2 jit_solution(16513834605540584680)
XLA Ops:
  0.0 0.0 copy-start
  0.0 0.9 %copy-done = bf16[2,128,512]{2,1,0:T(8,128)(2,1)S(1)} copy-done((bf16[2,128,512]{2,1,0:T(8,128)(2,1)S(1)}, bf16[2,128,512]{2,1,0:T(8,128)(2,1)}, u32[]{:S(2)}) %copy-start) | copy-done | bytes 262168
  1.0 0.0 copy-start.1
  1.0 0.9 %copy-done.1 = bf16[2,128,512]{2,1,0:T(8,128)(2,1)S(1)} copy-done((bf16[2,128,512]{2,1,0:T(8,128)(2,1)S(1)}, bf16[2,128,512]{2,1,0:T(8,128)(2,1)}, u32[]{:S(2)}) %copy-start.1) | copy-done | bytes 262168
  1.9 0.0 copy-start.2
  1.9 0.7 copy-done.2
  2.6 0.0 copy-start.3
  2.6 0.7 copy-done.3
  3.2 63.0 %shard_map.55 = bf16[128,3584]{1,0:T(8,128)(2,1)S(1)} custom-call(bf16[128,3584]{1,0:T(8,128)(2,1)} %queries.1, bf16[2,128,512]{2,1,0:T(8,128)(2,1)S(1)} %copy-done, bf16[2,128,512]{2,1,0:T(8,128)(2,1)S(1)} %copy-done.1, s32[64]{0:T(128)S(1)} %copy-done.2, s32[64]{0:T(128)S(1)} %copy-done.3), custom_call_target="tpu_custom_call" | custom-call | tf_op jit(solution)/shard_map/pallas_call | solution.py:285
  66.2 0.9 %copy.7 = bf16[128,3584]{1,0:T(8,128)(2,1)} copy(bf16[128,3584]{1,0:T(8,128)(2,1)S(1)} %shard_map.55) | data formatting | bytes 1835008
Async XLA Ops:
  0.0 0.9 %copy-start = (bf16[2,128,512]{2,1,0:T(8,128)(2,1)S(1)}, bf16[2,128,512]{2,1,0:T(8,128)(2,1)}, u32[]{:S(2)}) copy-start(bf16[2,128,512]{2,1,0:T(8,128)(2,1)} %branch.1) | copy-start | bytes 786436
  1.0 0.9 %copy-start.1 = (bf16[2,128,512]{2,1,0:T(8,128)(2,1)S(1)}, bf16[2,128,512]{2,1,0:T(8,128)(2,1)}, u32[]{:S(2)}) copy-start(bf16[2,128,512]{2,1,0:T(8,128)(2,1)} %prompt.1) | copy-start | bytes 786436
  1.9 0.7 copy-start.2
  2.6 0.7 copy-start.3

commit v3 on v2

--- a/solution.py
+++ b/solution.py
@@ -160,21 +160,37 @@
     def score(q, keys):
         return lax.dot_general(q, keys, (((1,), (1,)), ((), ())), preferred_element_type=jnp.float32)
 
-    def attend(slot, chunks, first=False, last=False):
-        q = jnp.concatenate([q_buf[slot, :, g * HEAD:(g + 1) * HEAD] for g in range(GROUP)], axis=0)
-        if first:
-            m, l, a = jnp.full((ROWS, HEAD), LOWEST, jnp.float32), jnp.zeros((ROWS, HEAD), jnp.float32), jnp.zeros((ROWS, HEAD), jnp.float32)
-        else:
-            m, l, a = top[slot], total[slot], acc[slot]
-
-        def scores_of(chunk):
-            buffer, start, length = chunk
+    def begin(slot):
+        return jnp.full((ROWS, HEAD), LOWEST, jnp.float32), jnp.zeros((ROWS, HEAD), jnp.float32), jnp.zeros((ROWS, HEAD), jnp.float32)
+
+    def resume(slot):
+        return top[slot], total[slot], acc[slot]
+
+    def keep(slot, m, l, a):
+        top[slot], total[slot], acc[slot] = m, l, a
+
+    def finish(slot, m, l, a):
+        mine = lax.rem(x - shift_of(slot) + LINE, LINE)
+        live = lax.broadcasted_iota(jnp.int32, (BLOCK, HEAD), 0) < counts[line + mine]
+        for g in range(GROUP):
+            rows = slice(g * BLOCK, (g + 1) * BLOCK)
+            stage[slot, :, g * HEAD:(g + 1) * HEAD] = jnp.where(live, a[rows] / l[rows], 0.0).astype(stage.dtype)
+
+    def attend(slots, chunks, load=resume, store=keep):
+        tasks = [(slot, n) for slot in slots for n in range(len(chunks))]
+
+        def scores_of(slot, n):
+            buffer, start, length = chunks[n]
+            q = jnp.concatenate([q_buf[slot, :, g * HEAD:(g + 1) * HEAD] for g in range(GROUP)], axis=0)
             s = score(q, buffer[0, pl.ds(start, length), :])
             return masked(s, slot) if buffer is tree else s
 
-        s = scores_of(chunks[0])
-        for n, (buffer, start, length) in enumerate(chunks):
-            following = scores_of(chunks[n + 1]) if n + 1 < len(chunks) else None
+        s = scores_of(*tasks[0])
+        for task, (slot, n) in enumerate(tasks):
+            following = scores_of(*tasks[task + 1]) if task + 1 < len(tasks) else None
+            buffer, start, length = chunks[n]
+            if n == 0:
+                m, l, a = load(slot)
             new = jnp.maximum(m, jnp.broadcast_to(jnp.max(s, axis=1, keepdims=True), (ROWS, HEAD)))
             factor = jnp.exp2((m - new) * TO_EXP2)
             weights = jnp.concatenate(
@@ -184,14 +200,8 @@
             a = a * factor + both[:, :HEAD]
             l = l * factor + both[:, HEAD:]
             m, s = new, following
-        if not last:
-            top[slot], total[slot], acc[slot] = m, l, a
-            return
-        mine = lax.rem(x - shift_of(slot) + LINE, LINE)
-        live = lax.broadcasted_iota(jnp.int32, (BLOCK, HEAD), 0) < counts[line + mine]
-        for g in range(GROUP):
-            rows = slice(g * BLOCK, (g + 1) * BLOCK)
-            stage[slot, :, g * HEAD:(g + 1) * HEAD] = jnp.where(live, a[rows] / l[rows], 0.0).astype(stage.dtype)
+            if n == len(chunks) - 1:
+                store(slot, m, l, a)
 
     def chunks(*lengths):
         start, found = lengths[0], []
@@ -200,63 +210,45 @@
             start += length
         return found
 
-    first = chunks(0, 768)
-    second = chunks(768, 768, 768) + [(tree, 0, LINE * BLOCK)]
-    third = chunks(2304, 768, 768, 768)
-    fourth = chunks(4608, 1024, 1024, 1024, 512)
-
     relay(0, NEAR)
     relay(0, FAR)
     query_copy(3).start()
-    for slot in (1, 2, 3):
-        tree_copy(slot).start()
     own_query.wait()
-    attend(0, first, first=True)
+    attend([0], chunks(0, 384, 384), load=begin)
     for slot in (1, 2, 3):
         prompt_copy(slot).wait_recv()
     for peer in NEAR + FAR:
         peer_copy(1, peer).start()
+    attend([0], chunks(768, 512))
     for slot in (1, 2):
         query_copy(slot).wait_recv()
-
-    def near_first(i, c):
-        attend(i + 1, first, first=True)
-        return c
-
-    lax.fori_loop(0, 2, near_first, 0)
+    for slot in (1, 2, 3):
+        tree_copy(slot).start()
+    attend([1, 2], chunks(0, 512, 768), load=begin)
     for peer in range(PEERS):
         for turn in range(3):
             relay_copy(0, peer, turn).wait_recv()
+    attend([0, 1, 2], chunks(1280, 1024))
+    relay(1, NEAR)
+    query_copy(3).wait_recv()
+    attend([3], chunks(0, 512, 768, 1024), load=begin)
+    relay(1, FAR)
     own_tree.wait()
     for slot in (1, 2, 3):
         tree_copy(slot).wait_recv()
 
-    def near_second(i, c):
-        attend(i, second)
-
-        @pl.when(i == 1)
-        def _():
-            relay(1, NEAR)
-
+    def middle(i, c):
+        attend([i], chunks(2304, 768, 768, 768) + [(tree, 0, LINE * BLOCK)])
         return c
 
-    lax.fori_loop(0, 3, near_second, 0)
-    query_copy(3).wait_recv()
-    attend(3, first + second, first=True)
-    relay(1, FAR)
-
-    def all_third(i, c):
-        attend(i, third)
-        return c
-
-    lax.fori_loop(0, LINE, all_third, 0)
+    lax.fori_loop(0, LINE, middle, 0)
     for peer in range(PEERS):
         for turn in range(3):
             relay_copy(1, peer, turn).wait_recv()
 
     def final(i, c):
         slot = 3 - i
-        attend(slot, fourth, last=True)
+        attend([slot], chunks(4608, 1024, 1024, 1024, 512), store=finish)
 
         @pl.when(i < 3)
         def _():
@@ -303,7 +295,7 @@
             pltpu.SemaphoreType.DMA((7,)),
         ],
         compiler_params=pltpu.CompilerParams(
-            collective_id=0, has_side_effects=True, vmem_limit_bytes=52 * 2**20
+            collective_id=0, has_side_effects=True, vmem_limit_bytes=60 * 2**20
         ),
     )(queries, branch, prompt, parents, counts)
 

time: 67.3 us -> 61.5 us (0.914)
  Pallas kernels: 63 us -> 59.2 us
  local copies, waits for them, and re-layouts: 4.13 us -> 2.16 us
    pallas_call x1, Pallas kernels: 63 us -> 59.2 us  [shards(): pl.pallas_call(kernel, out_shape=jax.ShapeDtypeStruct(queries.shape, quer...]
    unnamed x9 -> x1, local copies, waits for them, and re-layouts: 4.13 us -> 2.16 us
where the time goes in v3:
time: 61.5 us; the launch traced here: 61.4 us
  Pallas kernels  59.2 us (96%)
  local copies, waits for them, and re-layouts  2.16 us (4%)
    pallas_call x1, Pallas kernels, shards(): pl.pallas_call(kernel, out_shape=jax.ShapeDtypeStruct(queries.shape, quer...  59.2 us
    unnamed x1, local copies, waits for them, and re-layouts  2.16 us

profile of v3, /device:TPU:0, one launch (start us, length us, event | category | flops | bytes accessed | tf_op | source)
XLA Modules:
  0.0 61.4 jit_solution(4718964576689677741)
XLA Ops:
  0.0 59.2 %shard_map.55 = bf16[128,3584]{1,0:T(8,128)(2,1)} custom-call(bf16[128,3584]{1,0:T(8,128)(2,1)} %queries.1, bf16[2,128,512]{2,1,0:T(8,128)(2,1)} %branch.1, bf16[2,128,512]{2,1,0:T(8,128)(2,1)} %prompt.1, s32[64]{0:T(128)} %parents_in.1, s32[64]{0:T(128)} %counts_in.1), custom_call_target="tpu_custom_call" | custom-call | tf_op jit(solution)/shard_map/pallas_call | solution.py:277
  59.2 2.2 %copy.7 = bf16[128,3584]{1,0:T(8,128)(2,1)} copy(bf16[128,3584]{1,0:T(8,128)(2,1)} %shard_map.55) | data formatting | bytes 1835008

commit v4 on v3

--- a/solution.py
+++ b/solution.py
@@ -106,7 +106,7 @@
     def relay_copy(rest, peer, turn):
         half = (REST if rest else BLOCK) // 2
         start = (AT_REST_PEERS if rest else AT_PEERS) + (2 * peer + peer // 3) * half
-        index = 3 * peer + turn
+        index = 3 * (0, 2, 4, 1, 3, 5)[peer] + turn
         sem = (SEM_REST_RELAYS if rest else SEM_RELAYS) + index
         to = (AT_REST_RELAYS if rest else AT_RELAYS) + index * half
         return pltpu.make_async_remote_copy(
@@ -242,21 +242,22 @@
         return c
 
     lax.fori_loop(0, LINE, middle, 0)
-    for peer in range(PEERS):
+    for peer in NEAR:
         for turn in range(3):
             relay_copy(1, peer, turn).wait_recv()
-
-    def final(i, c):
+    attend([3, 2, 1], chunks(4608, 1024))
+    for peer in FAR:
+        for turn in range(3):
+            relay_copy(1, peer, turn).wait_recv()
+
+    def last(i, c):
         slot = 3 - i
-        attend([slot], chunks(4608, 1024, 1024, 1024, 512), store=finish)
-
-        @pl.when(i < 3)
-        def _():
-            out_copy(slot).start()
-
+        attend([slot], chunks(5632, 1024, 1024, 512), store=finish)
+        out_copy(slot).start()
         return c
 
-    lax.fori_loop(0, 4, final, 0)
+    lax.fori_loop(0, LINE - 1, last, 0)
+    attend([0], chunks(4608, 1024, 1024, 1024, 512), store=finish)
     own_out.start()
     for slot in (1, 2, 3):
         prompt_copy(slot).wait_send()

time: 61.5 us -> 61.4 us (level)
  no operation moved by 1% of the time
where the time goes in v4:
time: 61.4 us; the launch traced here: 61.2 us
  Pallas kernels  59 us (96%)
  local copies, waits for them, and re-layouts  2.16 us (4%)
    pallas_call x1, Pallas kernels, shards(): pl.pallas_call(kernel, out_shape=jax.ShapeDtypeStruct(queries.shape, quer...  59 us
    unnamed x1, local copies, waits for them, and re-layouts  2.16 us

profile of v4, /device:TPU:0, one launch (start us, length us, event | category | flops | bytes accessed | tf_op | source)
XLA Modules:
  0.0 61.2 jit_solution(9132656959758934266)
XLA Ops:
  0.0 59.0 %shard_map.55 = bf16[128,3584]{1,0:T(8,128)(2,1)} custom-call(bf16[128,3584]{1,0:T(8,128)(2,1)} %queries.1, bf16[2,128,512]{2,1,0:T(8,128)(2,1)} %branch.1, bf16[2,128,512]{2,1,0:T(8,128)(2,1)} %prompt.1, s32[64]{0:T(128)} %parents_in.1, s32[64]{0:T(128)} %counts_in.1), custom_call_target="tpu_custom_call" | custom-call | tf_op jit(solution)/shard_map/pallas_call | solution.py:278
  59.0 2.2 %copy.7 = bf16[128,3584]{1,0:T(8,128)(2,1)} copy(bf16[128,3584]{1,0:T(8,128)(2,1)} %shard_map.55) | data formatting | bytes 1835008
